TPU v7x, 32 devices: a whole 2x2x4 slice. The times are simulated.
32 devices in a mesh: dp: 2 (over x), head: 4 (over y, core), blk: 4 (over z).
Axes of the slice: x: 2, y: 2, z: 4, core: 2. Of those that a mesh axis runs over, the one named last changes fastest.
Arguments:
- tokens: bfloat16 [4, 2048, 768], P('dp', ('blk', 'head')), may hold values from -6 to 6
- segments: int32 [4, 2048], P('dp', ('blk', 'head')), may hold values from 0 to 255, as said below
- qkv_weight: bfloat16 [768, 2304], P(('dp', 'head', 'blk')), may hold values from -0.21875 to 0.21875
- qv_bias: bfloat16 [1536], P(('dp', 'head', 'blk')), may hold values from -3 to 3
- out_weight: bfloat16 [768, 768], P(('dp', 'head', 'blk')), may hold values from -9 to 9
- out_bias: bfloat16 [768], P(('dp', 'head', 'blk')), may hold values from -3 to 3
- attn_gain: bfloat16 [768], P(('dp', 'head', 'blk')), may hold values from 0.5 to 1.5
- attn_shift: bfloat16 [768], P(('dp', 'head', 'blk')), may hold values from -3 to 3
- up_weight: bfloat16 [768, 3072], P(('dp', 'head', 'blk')), may hold values from -0.21875 to 0.21875
- up_bias: bfloat16 [3072], P(('dp', 'head', 'blk')), may hold values from -3 to 3
- down_weight: bfloat16 [3072, 768], P(('dp', 'head', 'blk')), may hold values from -0.109375 to 0.109375
- down_bias: bfloat16 [768], P(('dp', 'head', 'blk')), may hold values from -3 to 3
- ffn_gain: bfloat16 [768], P(('dp', 'head', 'blk')), may hold values from 0.5 to 1.5
- ffn_shift: bfloat16 [768], P(('dp', 'head', 'blk')), may hold values from -3 to 3
- cotangent: bfloat16 [4, 2048, 768], P('dp', ('blk', 'head')), may hold values from -6 to 6
Outputs:
- layer_out: bfloat16 [4, 2048, 768], P('dp', ('blk', 'head'))
- grad_tokens: float32 [4, 2048, 768], P('dp', ('blk', 'head'))
- grad_qkv_weight: float32 [768, 2304], P(('dp', 'head', 'blk'))
- grad_qv_bias: float32 [1536], P(('dp', 'head', 'blk'))
- grad_out_weight: float32 [768, 768], P(('dp', 'head', 'blk'))
- grad_out_bias: float32 [768], P(('dp', 'head', 'blk'))
- grad_attn_gain: float32 [768], P(('dp', 'head', 'blk'))
- grad_attn_shift: float32 [768], P(('dp', 'head', 'blk'))
- grad_up_weight: float32 [768, 3072], P(('dp', 'head', 'blk'))
- grad_up_bias: float32 [3072], P(('dp', 'head', 'blk'))
- grad_down_weight: float32 [3072, 768], P(('dp', 'head', 'blk'))
- grad_down_bias: float32 [768], P(('dp', 'head', 'blk'))
- grad_ffn_gain: float32 [768], P(('dp', 'head', 'blk'))
- grad_ffn_shift: float32 [768], P(('dp', 'head', 'blk'))
Inputs may be any that keep to these rules, and one draw needn't show every extreme that they name: `segments`: along each row segment numbers never fall; each row ends in one or more padding tokens with segment number 256 - 1. Of the 2 rows of each index of dp, one holds a document that begins within its first 512 positions and ends within its last 512, with documents of under 512 tokens before and after it; the others hold documents of 200 to 2000 tokens, the last one before the padding possibly shorter.
All inputs are finite; a program needn't handle non-finite values.
Results may differ from a plain program's by a relative error of at most 0.017.
Values may be sent and summed in bfloat16 or wider, within the bound.
A program may use at most 192 MiB of HBM per device.

v0:
```python
import math

import jax
import jax.numpy as jnp
from jax import lax
from jax.experimental import pallas as pl
from jax.experimental.pallas import tpu as pltpu
from jax.sharding import PartitionSpec as P

HEADS = 12
HDIM = 64
NSEG = 256


EPS = 1e-12
MASKED = -1e30
SCALE = 0.125


def norm_forward(values_in, gain, shift):
    mean_val = jnp.mean(values_in, axis=-1, keepdims=True)
    centred = values_in - mean_val
    inv_std = lax.rsqrt(jnp.mean(centred * centred, axis=-1, keepdims=True) + EPS)
    normed = centred * inv_std
    return (normed * gain + shift, normed, inv_std)


def norm_backward(grad_in, normed, inv_std, gain):
    scaled = grad_in * gain
    inner_term = (
        scaled
        - jnp.mean(scaled, axis=-1, keepdims=True)
        - normed * jnp.mean(scaled * normed, axis=-1, keepdims=True)
    )
    return (inner_term * inv_std, jnp.sum(grad_in * normed, axis=0), jnp.sum(grad_in, axis=0))


def exact_gelu(values_in):
    return jax.nn.gelu(values_in, approximate=False)


def stretch_scores(queries, key_part, query_seg, key_seg, query_place, key_place):
    scores = (
        jnp.einsum("sqhd,skhd->shqk", queries, key_part, preferred_element_type=jnp.float32) * SCALE
    )
    same_doc = query_seg[:, None, :, None] == key_seg[:, None, None, :]
    own_place = query_place[:, None] == key_place[None, :]
    usable = (query_seg[:, None, :, None] != NSEG - 1) | own_place[None, None]
    return (scores, same_doc & usable)


def slice_keys(key_piece, value_piece, seg_piece, offset, step_rows):
    key_part = lax.dynamic_slice_in_dim(key_piece, offset, step_rows, 1)
    value_part = lax.dynamic_slice_in_dim(value_piece, offset, step_rows, 1)
    seg_part = lax.dynamic_slice_in_dim(seg_piece, offset, step_rows, 1)
    return (key_part, value_part, seg_part)


def part_grads(
    queries,
    grad_ctx,
    log_total,
    row_delta,
    query_seg,
    query_place,
    key_part,
    value_part,
    key_seg,
    key_place,
):
    scores, allowed = stretch_scores(queries, key_part, query_seg, key_seg, query_place, key_place)
    probs = jnp.where(allowed, jnp.exp(scores - log_total[..., None]), 0.0)
    grad_probs = jnp.einsum(
        "sqhd,skhd->shqk", grad_ctx, value_part, preferred_element_type=jnp.float32
    )
    grad_scores = (probs * (grad_probs - row_delta[..., None])).astype(jnp.bfloat16)
    grad_query = (
        jnp.einsum("shqk,skhd->sqhd", grad_scores, key_part, preferred_element_type=jnp.float32)
        * SCALE
    )
    grad_key = (
        jnp.einsum("shqk,sqhd->skhd", grad_scores, queries, preferred_element_type=jnp.float32)
        * SCALE
    )
    grad_value = jnp.einsum(
        "shqk,sqhd->skhd", probs.astype(jnp.bfloat16), grad_ctx, preferred_element_type=jnp.float32
    )
    return (grad_query, grad_key, grad_value)


def general_body(
    tokens,
    segments,
    qkv_weight,
    qv_bias,
    out_weight,
    out_bias,
    attn_gain,
    attn_shift,
    up_weight,
    up_bias,
    down_weight,
    down_bias,
    ffn_gain,
    ffn_shift,
    cotangent,
):
    seq_count, local_rows, model_width = tokens.shape
    group_count = lax.axis_size("head")
    group_width = model_width // group_count
    heads_here = HEADS // group_count
    block_rows = local_rows * group_count
    key_rows = block_rows * lax.axis_size("blk")
    token_count = seq_count * local_rows
    gathered = (
        lax.all_gather(qkv_weight, ("dp", "head", "blk"), axis=0, tiled=True),
        lax.all_gather(qv_bias, ("dp", "head", "blk"), axis=0, tiled=True),
        lax.all_gather(out_weight, ("dp", "head", "blk"), axis=0, tiled=True),
        lax.all_gather(out_bias, ("dp", "head", "blk"), axis=0, tiled=True),
        lax.all_gather(attn_gain, ("dp", "head", "blk"), axis=0, tiled=True),
        lax.all_gather(attn_shift, ("dp", "head", "blk"), axis=0, tiled=True),
        lax.all_gather(up_weight, ("dp", "head", "blk"), axis=0, tiled=True),
        lax.all_gather(up_bias, ("dp", "head", "blk"), axis=0, tiled=True),
        lax.all_gather(down_weight, ("dp", "head", "blk"), axis=0, tiled=True),
        lax.all_gather(down_bias, ("dp", "head", "blk"), axis=0, tiled=True),
        lax.all_gather(ffn_gain, ("dp", "head", "blk"), axis=0, tiled=True),
        lax.all_gather(ffn_shift, ("dp", "head", "blk"), axis=0, tiled=True),
    )
    (
        whole_qkv,
        whole_qv,
        whole_out,
        whole_out_bias,
        whole_attn_gain,
        whole_attn_shift,
        whole_up,
        whole_up_bias,
        whole_down,
        whole_down_bias,
        whole_ffn_gain,
        whole_ffn_shift,
    ) = gathered
    attn_scale = whole_attn_gain.astype(jnp.float32)
    ffn_scale = whole_ffn_gain.astype(jnp.float32)
    flat_tokens = tokens.reshape(token_count, model_width)
    mixed = jnp.dot(flat_tokens, whole_qkv, preferred_element_type=jnp.float32)
    bias_row = jnp.concatenate(
        [whole_qv[:model_width], jnp.zeros((model_width,), jnp.bfloat16), whole_qv[model_width:]]
    ).astype(jnp.float32)
    mixed_low = (mixed + bias_row).astype(jnp.bfloat16)
    grouped = (
        mixed_low.reshape(seq_count, local_rows, 3, group_count, group_width)
        .transpose(0, 1, 3, 2, 4)
        .reshape(seq_count, local_rows, group_count, 3 * group_width)
    )
    seg_copies = jnp.broadcast_to(
        segments.astype(jnp.bfloat16)[:, :, None, None], (seq_count, local_rows, group_count, 1)
    )
    arrived, seg_arrived = (
        lax.all_to_all(grouped, "head", split_axis=2, concat_axis=1, tiled=True),
        lax.all_to_all(seg_copies, "head", split_axis=2, concat_axis=1, tiled=True),
    )
    arrived = arrived.reshape(seq_count, block_rows, 3, heads_here, HDIM)
    queries = arrived[:, :, 0]
    keys_here = arrived[:, :, 1]
    values_here = arrived[:, :, 2]
    query_seg = seg_arrived.reshape(seq_count, block_rows)
    query_place = lax.axis_index("blk") * block_rows + jnp.arange(block_rows)
    row_shape = (seq_count, heads_here, block_rows)
    start_state = (
        jnp.full(row_shape, MASKED, jnp.float32),
        jnp.zeros(row_shape, jnp.float32),
        jnp.zeros(row_shape + (HDIM,), jnp.float32),
    )
    key_piece = lax.all_gather(keys_here, "blk", axis=1, tiled=True)
    value_piece = lax.all_gather(values_here, "blk", axis=1, tiled=True)
    seg_piece = lax.all_gather(query_seg, "blk", axis=1, tiled=True)
    piece_rows = key_piece.shape[1]
    step_rows = math.gcd(piece_rows, 512)

    def attend_one_step(state_in, step_index):
        offset = step_index * step_rows
        key_part, value_part, key_seg = slice_keys(
            key_piece, value_piece, seg_piece, offset, step_rows
        )
        key_place = offset + jnp.arange(step_rows)
        best, total, accum = state_in
        scores, allowed = stretch_scores(
            queries, key_part, query_seg, key_seg, query_place, key_place
        )
        new_best = jnp.maximum(best, jnp.max(jnp.where(allowed, scores, MASKED), axis=-1))
        weights = jnp.where(allowed, jnp.exp(scores - new_best[..., None]), 0.0)
        factor = jnp.exp(best - new_best)
        total = total * factor + jnp.sum(weights, axis=-1)
        accum = accum * factor[..., None] + jnp.einsum(
            "shqk,skhd->shqd",
            weights.astype(jnp.bfloat16),
            value_part,
            preferred_element_type=jnp.float32,
        )
        return ((new_best, total, accum), None)

    result, unused = lax.scan(attend_one_step, start_state, jnp.arange(piece_rows // step_rows))
    best, total, accum = result
    context = accum / total[..., None]
    log_total = best + jnp.log(total)
    context_low = (
        context.astype(jnp.bfloat16)
        .transpose(0, 2, 1, 3)
        .reshape(seq_count, block_rows, 1, group_width)
    )
    returned_ctx = lax.all_to_all(context_low, "head", split_axis=1, concat_axis=2, tiled=True)
    ctx_tokens = returned_ctx.reshape(token_count, model_width)
    attended = jnp.dot(
        ctx_tokens, whole_out, preferred_element_type=jnp.float32
    ) + whole_out_bias.astype(jnp.float32)
    first_sum = flat_tokens.astype(jnp.float32) + attended
    hidden, normed_one, inv_one = norm_forward(
        first_sum, attn_scale, whole_attn_shift.astype(jnp.float32)
    )
    hidden_low = hidden.astype(jnp.bfloat16)
    inner = jnp.dot(
        hidden_low, whole_up, preferred_element_type=jnp.float32
    ) + whole_up_bias.astype(jnp.float32)
    active, gelu_pull = jax.vjp(exact_gelu, inner)
    active_low = active.astype(jnp.bfloat16)
    branch = jnp.dot(
        active_low, whole_down, preferred_element_type=jnp.float32
    ) + whole_down_bias.astype(jnp.float32)
    final, normed_two, inv_two = norm_forward(
        hidden + branch, ffn_scale, whole_ffn_shift.astype(jnp.float32)
    )
    layer_out = final.astype(jnp.bfloat16).reshape(seq_count, local_rows, model_width)
    grad_final = cotangent.reshape(token_count, model_width).astype(jnp.float32)
    grad_second, grad_ffn_gain, grad_ffn_shift = norm_backward(
        grad_final, normed_two, inv_two, ffn_scale
    )
    grad_branch = grad_second.astype(jnp.bfloat16)
    grad_down = jnp.dot(active_low.T, grad_branch, preferred_element_type=jnp.float32)
    grad_down_bias = jnp.sum(grad_branch.astype(jnp.float32), axis=0)
    grad_active = jnp.dot(grad_branch, whole_down.T, preferred_element_type=jnp.float32)
    grad_inner = gelu_pull(grad_active)[0].astype(jnp.bfloat16)
    grad_up = jnp.dot(hidden_low.T, grad_inner, preferred_element_type=jnp.float32)
    grad_up_bias = jnp.sum(grad_inner.astype(jnp.float32), axis=0)
    grad_hidden = grad_second + jnp.dot(grad_inner, whole_up.T, preferred_element_type=jnp.float32)
    grad_first, grad_attn_gain, grad_attn_shift = norm_backward(
        grad_hidden, normed_one, inv_one, attn_scale
    )
    grad_attended = grad_first.astype(jnp.bfloat16)
    grad_out = jnp.dot(ctx_tokens.T, grad_attended, preferred_element_type=jnp.float32)
    grad_out_bias = jnp.sum(grad_attended.astype(jnp.float32), axis=0)
    grad_context = jnp.dot(grad_attended, whole_out.T, preferred_element_type=jnp.float32).astype(
        jnp.bfloat16
    )
    grad_sent = lax.all_to_all(
        grad_context.reshape(seq_count, local_rows, group_count, group_width),
        "head",
        split_axis=2,
        concat_axis=1,
        tiled=True,
    )
    grad_ctx = grad_sent.reshape(seq_count, block_rows, heads_here, HDIM)
    row_delta = jnp.einsum("sqhd,shqd->shq", grad_ctx.astype(jnp.float32), context)
    query_zero = jnp.zeros((seq_count, block_rows, heads_here, HDIM), jnp.float32)
    zero_keys = jnp.zeros((seq_count, key_rows, heads_here, HDIM), jnp.float32)
    gather_key_piece = lax.all_gather(keys_here, "blk", axis=1, tiled=True)
    gather_value_piece = lax.all_gather(values_here, "blk", axis=1, tiled=True)
    gather_seg_piece = lax.all_gather(query_seg, "blk", axis=1, tiled=True)
    piece_rows = gather_key_piece.shape[1]
    gather_step_rows = math.gcd(piece_rows, 512)

    def gather_one_step(state_in, step_index):
        offset = step_index * gather_step_rows
        key_part, value_part, key_seg = slice_keys(
            gather_key_piece, gather_value_piece, gather_seg_piece, offset, gather_step_rows
        )
        key_place = offset + jnp.arange(gather_step_rows)
        grad_q, grad_k, grad_v = state_in
        part_q, part_k, part_v = part_grads(
            queries,
            grad_ctx,
            log_total,
            row_delta,
            query_seg,
            query_place,
            key_part,
            value_part,
            key_seg,
            key_place,
        )
        grad_k = lax.dynamic_update_slice_in_dim(
            grad_k,
            lax.dynamic_slice_in_dim(grad_k, offset, gather_step_rows, 1) + part_k,
            offset,
            1,
        )
        grad_v = lax.dynamic_update_slice_in_dim(
            grad_v,
            lax.dynamic_slice_in_dim(grad_v, offset, gather_step_rows, 1) + part_v,
            offset,
            1,
        )
        return ((grad_q + part_q, grad_k, grad_v), None)

    result, unused = lax.scan(
        gather_one_step,
        (query_zero, zero_keys, zero_keys),
        jnp.arange(piece_rows // gather_step_rows),
    )
    grad_q, all_keys, all_values = result
    grad_k, grad_v = (
        lax.psum_scatter(
            all_keys.astype(jnp.bfloat16), "blk", scatter_dimension=1, tiled=True
        ).astype(jnp.float32),
        lax.psum_scatter(
            all_values.astype(jnp.bfloat16), "blk", scatter_dimension=1, tiled=True
        ).astype(jnp.float32),
    )
    grad_low = jnp.concatenate(
        [
            grad_q.astype(jnp.bfloat16).reshape(seq_count, block_rows, 1, group_width),
            grad_k.astype(jnp.bfloat16).reshape(seq_count, block_rows, 1, group_width),
            grad_v.astype(jnp.bfloat16).reshape(seq_count, block_rows, 1, group_width),
        ],
        axis=3,
    )
    back_tokens = lax.all_to_all(grad_low, "head", split_axis=1, concat_axis=2, tiled=True)
    grad_mixed = (
        back_tokens.reshape(seq_count, local_rows, group_count, 3, group_width)
        .transpose(0, 1, 3, 2, 4)
        .reshape(token_count, 3 * model_width)
    )
    grad_qkv = jnp.dot(flat_tokens.T, grad_mixed, preferred_element_type=jnp.float32)
    column_sums = jnp.sum(grad_mixed.astype(jnp.float32), axis=0)
    grad_qv = jnp.concatenate([column_sums[:model_width], column_sums[2 * model_width :]])
    grad_tokens = grad_first + jnp.dot(grad_mixed, whole_qkv.T, preferred_element_type=jnp.float32)
    summed = (
        lax.psum_scatter(grad_qkv, ("dp", "head", "blk"), scatter_dimension=0, tiled=True),
        lax.psum_scatter(grad_qv, ("dp", "head", "blk"), scatter_dimension=0, tiled=True),
        lax.psum_scatter(grad_out, ("dp", "head", "blk"), scatter_dimension=0, tiled=True),
        lax.psum_scatter(grad_out_bias, ("dp", "head", "blk"), scatter_dimension=0, tiled=True),
        lax.psum_scatter(grad_attn_gain, ("dp", "head", "blk"), scatter_dimension=0, tiled=True),
        lax.psum_scatter(grad_attn_shift, ("dp", "head", "blk"), scatter_dimension=0, tiled=True),
        lax.psum_scatter(grad_up, ("dp", "head", "blk"), scatter_dimension=0, tiled=True),
        lax.psum_scatter(grad_up_bias, ("dp", "head", "blk"), scatter_dimension=0, tiled=True),
        lax.psum_scatter(grad_down, ("dp", "head", "blk"), scatter_dimension=0, tiled=True),
        lax.psum_scatter(grad_down_bias, ("dp", "head", "blk"), scatter_dimension=0, tiled=True),
        lax.psum_scatter(grad_ffn_gain, ("dp", "head", "blk"), scatter_dimension=0, tiled=True),
        lax.psum_scatter(grad_ffn_shift, ("dp", "head", "blk"), scatter_dimension=0, tiled=True),
    )
    return (
        layer_out,
        grad_tokens.reshape(seq_count, local_rows, model_width),
        summed[0],
        summed[1],
        summed[2],
        summed[3],
        summed[4],
        summed[5],
        summed[6],
        summed[7],
        summed[8],
        summed[9],
        summed[10],
        summed[11],
    )


MESH = pl.DeviceIdType.MESH
ANY = pl.ANY
VMEM_LIMIT = 60 * 1024 * 1024


def remote(src, dst, send_sem, recv_sem, device):
    return pltpu.make_async_remote_copy(
        src_ref=src,
        dst_ref=dst,
        send_sem=send_sem,
        recv_sem=recv_sem,
        device_id=device,
        device_id_type=MESH,
    )


def wait_for(ref, sem):
    pltpu.make_async_copy(ref, ref, sem).wait()


def place():
    x, h, z = lax.axis_index("dp"), lax.axis_index("head"), lax.axis_index("blk")
    return x, lax.div(h, 2), lax.rem(h, 2), h, z


def greet(peers):
    barrier = pltpu.get_barrier_semaphore()
    for peer in peers:
        pl.semaphore_signal(barrier, inc=1, device_id=peer, device_id_type=MESH)
    pl.semaphore_wait(barrier, len(peers))


def peers_of(x, h, c, z):
    around = [(x, h, lax.rem(z + k, 4)) for k in (1, 2, 3)]
    other = lax.rem(h + 2, 4)
    beside = z + 1 - 2 * lax.rem(z, 2)
    return around + [(1 - x, h, z), (x, other, z), (x, other, beside), (x, h + 1 - 2 * c, z)]


def nt(left, right):
    return lax.dot_general(left, right, (((1,), (1,)), ((), ())), preferred_element_type=jnp.float32)


def tn(left, right):
    return lax.dot_general(left, right, (((0,), (0,)), ((), ())), preferred_element_type=jnp.float32)


def nn(left, right):
    return jnp.dot(left, right, preferred_element_type=jnp.float32)


def add_norm(values_in):
    mean_val = jnp.mean(values_in, axis=-1, keepdims=True)
    centred = values_in - mean_val
    inv_std = lax.rsqrt(jnp.mean(centred * centred, axis=-1, keepdims=True) + EPS)
    return centred * inv_std, inv_std


def norm_pull(scaled, normed, inv_std):
    return inv_std * (
        scaled
        - jnp.mean(scaled, axis=-1, keepdims=True)
        - normed * jnp.mean(scaled * normed, axis=-1, keepdims=True)
    )


def column_sum(values_in):
    return jnp.sum(values_in, axis=0, keepdims=True)


CUT = 1
EARLY = 0
AHEAD = 2
BESIDE_TOKENS = {
    99: ((0, 0), (0, 1)),
    100: ((1, 0),),
    101: ((1, 1), (1, 2)),
    102: ((1, 3),),
    104: ((1, 4),),
    111: ((1, 5),),
    112: ((1, 6),),
}
WQ_STEPS = (4, 5, 8)
SUB = 2
ROWS_SUB = 64
PIECES = (
    ("out", (24, 768), 0, 0),
    ("up", (24, 1536), 0, 0),
    ("up", (24, 1536), 0, 1536),
    ("down", (48, 768), 0, 0),
    ("down", (48, 768), 48, 0),
)


def forward_kernel(
    tokens,
    cot,
    segments,
    wqkv,
    wout,
    wup,
    wdown,
    rows24,
    up_bias,
    qv_bias,
    dr1,
    gvec,
    lo_out,
    dc_all,
    gout_h,
    gup_h,
    gdown_h,
    tok_all,
    q_all,
    k_all,
    v_all,
    o_all,
    lse_all,
    wq_all,
    idrow_all,
    idcol_all,
    tok,
    land,
    wqs,
    qs,
    ks,
    vs,
    os_,
    lses,
    idrow,
    idcol,
    ctx,
    wout_g,
    wup_g,
    wdown_g,
    win,
    ctx_in,
    cot_in,
    wout_v,
    wup_v,
    active,
    slope,
    go,
    gu,
    gd,
    ro,
    ru,
    rd,
    tok_rs,
    tz_ss,
    tx_ss,
    ty_ss,
    tc_ss,
    cot_ss,
    cot_rs,
    wq_ss,
    wq_rs,
    wz_ss,
    wz_rs,
    wp_ss,
    wp_rs,
    ctx_ss,
    ctx_rs,
    out_sem,
    c_ss,
    c_rs,
    o_sem,
    wq,
    lo,
    dctx,
    r2a,
    r2b,
    lo_ss,
    lo_rs,
    dc_ss,
    dc_rs,
    s2_ss,
    s2_rs,
):
    f32, bf = jnp.float32, jnp.bfloat16
    x, y, c, h, z = place()
    zl, pi = lax.rem(z, 2), lax.div(z, 2)
    g = 2 * zl + y
    me = x * 16 + h * 4 + z
    hy = lax.rem(h + 2, 4)
    hc = h + 1 - 2 * c
    to_x, to_y, to_c = (1 - x, h, z), (x, hy, z), (x, hc, z)
    pz, zc = z + 1 - 2 * zl, lax.rem(z + 2, 4)
    to_n, to_d, to_z = (x, h, pz), (x, hy, pz), (x, h, zc)
    mid = jnp.where(z < 2, 2, 1)
    inner = jnp.logical_or(z == 1, z == 2)
    outer = jnp.logical_not(inner)
    def moved(values, width, steps, index):
        out = None
        for k, start in enumerate(steps):
            ends = []
            if start:
                ends.append(jnp.zeros((values.shape[0], start), f32))
            ends.append(values)
            if width - start - values.shape[1]:
                ends.append(jnp.zeros((values.shape[0], width - start - values.shape[1]), f32))
            row = jnp.concatenate(ends, axis=1)
            out = row if out is None else jnp.where(index == k, row, out)
        return out

    starts = [48 * k for k in range(4)] + [384 + 48 * k for k in range(4)]
    bias_row = moved(qv_bias[...].astype(f32), 576, starts, 4 * x + z)
    six = moved(rows24[...].astype(f32), 128, [24 * k for k in range(4)], z)
    up_row = jnp.concatenate([up_bias[...].astype(f32), jnp.zeros((1, 32), f32)], axis=1)
    ten = [six[k : k + 1] for k in range(6)] + [jnp.where(z == k, up_row, 0.0) for k in range(4)]
    gap = jnp.zeros((1, 64), f32)
    none = jnp.zeros((1, 128), f32)
    slots = [
        jnp.concatenate(ten[0:4] + [gap], axis=1),
        jnp.concatenate(ten[4:8] + [gap], axis=1),
        jnp.concatenate(ten[8:10] + [none, none, gap], axis=1),
    ]
    seg_rows = segments[...].astype(f32)
    seg_rows = [jnp.concatenate([seg_rows[k : k + 1], jnp.zeros((1, 448), f32)], axis=1) for k in range(2)]
    last_rows = jnp.concatenate(slots + seg_rows + [jnp.zeros((2, 576), f32)], axis=0)
    whole = wqkv[...].astype(f32)
    for q in range(4):
        cols = [whole[:, 768 * p + 192 * q : 768 * p + 192 * q + 192] for p in range(3)]
        first_row = jnp.where(h == q, bias_row, 0.0)
        rows = [jnp.concatenate(cols, axis=1), first_row, last_rows]
        wq[q] = jnp.concatenate(rows, axis=0).astype(bf)
    greet(peers_of(x, h, c, z))

    mine = z * 4 + h
    weights = {"out": (wout, wout_g), "up": (wup, wup_g), "down": (wdown, wdown_g)}
    count = len(PIECES)
    base = x * 16 + h * 4
    bx, by = (1 - x) * 16 + h * 4, x * 16 + hy * 4

    def side(start, ab):
        return pl.ds(start, CUT) if ab == 0 else pl.ds(start + CUT, 4 - CUT)

    sa, sb = side(bx, 0), side(by, 1)

    def quad(xs, hs):
        return pl.ds(xs * 16 + hs * 4, 4)

    sent = []

    def shard(n):
        name, shape, row, col = PIECES[n]
        return weights[name][0].at[pl.ds(row, shape[0]), pl.ds(col, shape[1])]

    def at(n, where):
        name, shape, row, col = PIECES[n]
        return weights[name][1].at[where, pl.ds(row, shape[0]), pl.ds(col, shape[1])]

    def two(n):
        return at(n, pl.ds(0, 2))

    def some(n, ab):
        return at(n, side(0, ab))

    def pass_on(n, where, k, sem, dev):
        remote(at(n, where), at(n, where), wp_ss.at[n, k], wp_rs.at[(n,) + sem], dev).start()
        sent.append((n, k))

    def along_z(n):
        pltpu.make_async_copy(shard(n), at(n, me), wz_rs.at[n, z]).start()
        for k, zz in enumerate((pz, mid)):
            remote(shard(n), at(n, me), wz_ss.at[n, k], wz_rs.at[n, z], (x, h, zz)).start()

    def relay(n):
        @pl.when(inner)
        def _():
            there = pl.ds(base + jnp.where(z < 2, 2, 0), 2)
            for k in range(2):
                wait_for(at(n, 0), wz_rs.at[n, jnp.where(z < 2, 2, 0) + k])
            remote(at(n, there), at(n, there), wz_ss.at[n, 2], wz_rs.at[n, 4], (x, h, pz)).start()

    def first_hop(n):
        for k in range(2):
            wait_for(at(n, 0), wz_rs.at[n, jnp.where(z < 2, 0, 2) + k])

        @pl.when(outer)
        def _():
            wait_for(two(n), wz_rs.at[n, 4])

        for k, dev in enumerate((to_x, to_y, to_c)):
            pass_on(n, quad(x, h), k, (x, h, 0), dev)

    def second_hop(n):
        wait_for(at(n, quad(0, 0)), wp_rs.at[n, 1 - x, h, 0])
        wait_for(at(n, quad(0, 0)), wp_rs.at[n, x, hy, 0])
        pass_on(n, sa, 3, (1 - x, h, 0), to_y)
        pass_on(n, sb, 4, (x, hy, 1), to_x)
        pass_on(n, quad(1 - x, h), 5, (1 - x, h, 0), to_c)
        pass_on(n, quad(x, hy), 6, (x, hy, 0), to_c)

    def third_hop(n):
        for ab in range(2):
            wait_for(some(n, ab), wp_rs.at[n, 1 - x, hy, ab])
        pass_on(n, quad(1 - x, hy), 7, (1 - x, hy, 0), to_c)

    def advance(t):
        if t < count:
            first_hop(t)
        if t + AHEAD < count:
            relay(t + AHEAD)
        if 0 <= t - 1 < count:
            second_hop(t - 1)
        if 0 <= t - 2 < count:
            third_hop(t - 2)

    for n in range(EARLY):
        along_z(n)

    cuts = [pl.ds(ROWS_SUB * q, ROWS_SUB) for q in range(SUB)]

    def send_row(i, to):
        for q in range(SUB):
            remote(
                tokens.at[i, cuts[q]], tok.at[mine, cuts[q]], tz_ss.at[i, q], tok_rs.at[mine, q], to
            ).start()

    for i in range(2):

        @pl.when(pi == i)
        def _():
            send_row(i, to_n)
            for q in range(SUB):
                pltpu.make_async_copy(
                    tokens.at[i, cuts[q]], tok.at[mine, cuts[q]], tok_rs.at[mine, q]
                ).start()

        @pl.when(pi != i)
        def _():
            send_row(i, (x, h, 1 + i))

    def run_beside(t):
        for kind, n in BESIDE_TOKENS.get(t, ()):
            relay(n) if kind == 0 else advance(n)

    pltpu.make_async_copy(wq.at[g], land.at[c, x, pi, g], wq_rs.at[c, x, pi, g]).start()
    for k, (dev, target) in enumerate(
        ((to_n, 2 * (1 - zl) + y), (to_y, 2 * zl + 1 - y), (to_d, 2 * (1 - zl) + 1 - y))
    ):
        remote(wq.at[target], land.at[c, x, pi, g], wq_ss.at[k], wq_rs.at[c, x, pi, g], dev).start()

    def give_slices(xs, pp, k, dev):
        block = land.at[c, xs, pp]
        remote(block, block, wq_ss.at[k], wq_rs.at[c, xs, pp, 0], dev).start()

    for q in range(4):
        wait_for(land.at[c, x, pi, q], wq_rs.at[c, x, pi, q])
    give_slices(x, pi, 3, to_z)
    give_slices(x, pi, 4, to_x)
    give_slices(x, pi, 5, to_c)
    for n in range(EARLY, count):
        along_z(n)
    for i in range(2):

        @pl.when(pi == i)
        def _():
            pltpu.make_async_copy(cot.at[i], cot_in.at[pi], cot_rs.at[pi]).start()

        @pl.when(pi != i)
        def _():
            remote(cot.at[i], cot_in.at[pi], cot_ss, cot_rs.at[pi], to_z).start()

    turns = (z, pz, zc, lax.rem(pz + 2, 4))

    def hand_on(p, q, sends, keep_sem):
        wait_for(tok.at[p, cuts[q]], tok_rs.at[p, q])
        for sem, dev in sends:
            remote(tok.at[p, cuts[q]], tok.at[p, cuts[q]], sem.at[q], tok_rs.at[p, q], dev).start()
        if q == SUB - 1:
            remote(tok.at[p], tok.at[p], keep_sem, tok_rs.at[p, 0], to_c).start()

    def own_piece(k, q):
        p = turns[k] * 4 + h
        hand_on(p, q, [(ty_ss.at[k], to_y)], tc_ss.at[k])
        if k >= 2:

            @pl.when(inner)
            def _():
                cut = cuts[q]
                remote(
                    tok.at[p, cut], tok.at[p, cut], tx_ss.at[k, q], tok_rs.at[p, q], to_n
                ).start()

    def side_piece(k, q):
        hand_on(turns[k] * 4 + hy, q, [], tc_ss.at[4 + k])

    def slices_step(t):
        if t == WQ_STEPS[0]:
            wait_for(land.at[c, x, 1 - pi], wq_rs.at[c, x, 1 - pi, 0])
            give_slices(x, 1 - pi, 6, to_x)
            give_slices(x, 1 - pi, 7, to_c)
        for k in range(2):
            if t == WQ_STEPS[1 + k]:
                there = (pi, 1 - pi)[k]
                wait_for(land.at[c, 1 - x, there], wq_rs.at[c, 1 - x, there, 0])
                give_slices(1 - x, there, 8 + k, to_c)

    order = [(0, q) for q in range(SUB)] + [(k, q) for q in range(SUB) for k in range(1, 4)]
    lag = 3
    for t in range(len(order) + lag):
        if t < len(order):
            own_piece(*order[t])
        if t >= lag:
            side_piece(*order[t - lag])
        slices_step(t)
        run_beside(t)

    run_beside(99)
    for k in range(4):
        zz = lax.rem(z + k, 4)
        for hh in (hc, lax.rem(hc + 2, 4)):
            p = zz * 4 + hh
            wait_for(tok.at[p], tok_rs.at[p, 0])
    for k in range(4):
        wait_for(land.at[1 - c, k // 2, k % 2], wq_rs.at[1 - c, k // 2, k % 2, 0])

    run_beside(100)
    bias8 = jnp.zeros((8, 576), jnp.float32)
    for xs in range(2):
        for hs in range(4):
            part = []
            window = jnp.zeros((8, 576), jnp.float32)
            for zz in range(4):
                block = land[hs % 2, xs, zz // 2, 2 * (zz % 2) + hs // 2].astype(jnp.float32)
                part.append(block[:24])
                window = window + block[24:]
            start = (xs * 16 + hs * 4) * 24
            bias8 = bias8 + window
            win[xs * 4 + hs] = window
            wqs[start : start + 96, :] = jnp.concatenate(part, axis=0).astype(jnp.bfloat16)
    bias = bias8[0:1, :]

    lane = lax.broadcasted_iota(jnp.int32, (1, 128), 1)
    for p in range(16):
        zz, hs = p // 4, p % 4
        block = land[hs % 2, x, zz // 2, 2 * (zz % 2) + hs // 2].astype(jnp.float32)
        seg = jnp.where(pi == 0, block[28:29, :128], block[29:30, :128])
        ident = jnp.where(seg == NSEG - 1.0, (1000.0 + 128 * p) + lane.astype(f32), seg)
        idrow[:, 128 * p : 128 * p + 128] = jnp.broadcast_to(ident, (8, 128))
        idcol[128 * p : 128 * p + 128, :] = jnp.transpose(jnp.broadcast_to(ident, (128, 128)))

    def project(j, carry):
        zz, yy = lax.div(j, 2), lax.rem(j, 2)
        p = zz * 4 + yy * 2 + c
        rows = pl.ds(pl.multiple_of(j * 128, 128), 128)
        mixed = nn(tok[p], wqs[:, 0:192]) + bias[:, 0:192]
        low = mixed.astype(jnp.bfloat16) * jnp.bfloat16(SCALE)
        for hh in range(3):
            qs[hh, rows, :] = low[:, 64 * hh : 64 * hh + 64]
        both = tok[pl.ds(2 * j, 2)].reshape(256, 768)
        wide = nn(both, wqs[:, 192:576]) + bias[:, 192:576]
        wide = wide.astype(jnp.bfloat16)
        key_rows = pl.ds(pl.multiple_of(j * 256, 256), 256)
        for hh in range(3):
            ks[hh, key_rows, :] = wide[:, 64 * hh : 64 * hh + 64]
            vs[hh, key_rows, :] = wide[:, 192 + 64 * hh : 256 + 64 * hh]
        return carry

    lax.fori_loop(0, 8, project, 0)
    run_beside(101)

    def attend(zz):
        rows = slice(zz * 256, zz * 256 + 256)
        upper = pl.ds(pl.multiple_of((zz * 4 + c) * 128, 128), 128)
        lower = pl.ds(pl.multiple_of((zz * 4 + 2 + c) * 128, 128), 128)
        idq = jnp.concatenate([idcol[upper, :], idcol[lower, :]], axis=0)
        mask = idq[:, 0:1] == idrow[0:1, :]
        def one_head(hh, carry):
            scores = nt(qs[hh, rows, :], ks[hh])
            scores = jnp.where(mask, scores, MASKED)
            top = jnp.max(scores, axis=-1, keepdims=True)
            weights_ = jnp.exp(scores - top)
            total = jnp.sum(weights_, axis=-1, keepdims=True)
            o = nn(weights_.astype(jnp.bfloat16), vs[hh]) / total
            os_[hh, rows, :] = o
            lse = jnp.broadcast_to(top + jnp.log(total), (256, 128))
            lses[hh, :, rows] = jnp.transpose(lse)[0:8, :]
            return carry

        lax.fori_loop(0, 3, one_head, 0)
        out = jnp.concatenate([os_[k, rows, :] for k in range(3)], axis=1).astype(jnp.bfloat16)
        slot = zz // 2
        for yy in range(2):
            j = zz * 2 + yy
            ctx[j] = out[128 * yy : 128 * yy + 128]
            stay = jnp.logical_and(zl == zz % 2, y == yy)

            @pl.when(stay)
            def _():
                pltpu.make_async_copy(ctx.at[j], ctx_in.at[g, slot], ctx_rs.at[g, slot]).start()

            @pl.when(jnp.logical_not(stay))
            def _():
                remote(
                    ctx.at[j],
                    ctx_in.at[g, slot],
                    ctx_ss.at[j],
                    ctx_rs.at[g, slot],
                    (x, yy * 2 + c, 2 * pi + zz % 2),
                ).start()

    for t in range(4):
        attend(t)
        run_beside(102 + t)

    kept = (
        (tok, tok_all),
        (qs, q_all),
        (ks, k_all),
        (vs, v_all),
        (os_, o_all),
        (lses, lse_all),
        (wqs, wq_all),
        (idrow, idrow_all),
        (idcol, idcol_all),
    )
    for k, (src, dst) in enumerate(kept):
        pltpu.make_async_copy(src, dst, out_sem.at[k]).start()
    def arrive(n):
        for xs in range(2):
            for yy in range(2):
                wait_for(at(n, quad(0, 0)), wp_rs.at[n, xs, yy * 2 + 1 - c, 0])

    def flatten(src, dst, cols):
        for k in range(8):
            part = [src[4 * k + q, :, cols].astype(f32) for q in range(4)]
            dst[96 * k : 96 * k + 96, cols] = jnp.concatenate(part, axis=0).astype(bf)

    run_beside(110)
    for s in range(2):
        wait_for(cot_in.at[s], cot_rs.at[s])
        for q in range(4):
            wait_for(ctx_in.at[q, s], ctx_rs.at[q, s])
    arrive(0)
    def row(i):
        at_lane = 128 * (i % 4) if i < 6 else 0
        if i < 6:
            pieces = [win[w, 1 + i // 4 : 2 + i // 4, at_lane : at_lane + 96] for w in range(8)]
        else:
            pieces = []
            for w in (2 * (i - 6), 2 * (i - 6) + 1):
                for k in range(6, 10):
                    at_lane = 128 * (k % 4)
                    pieces.append(win[w, 1 + k // 4 : 2 + k // 4, at_lane : at_lane + 96])
        return jnp.concatenate(pieces, axis=1)

    full_ctx = jnp.concatenate([ctx_in[q].reshape(256, 192) for q in range(4)], axis=1)
    flatten(wout_g, wout_v, slice(0, 768))
    own = jnp.concatenate([tok[zl * 4 + h], tok[(2 + zl) * 4 + h]], axis=0).astype(f32)
    normed_one, inv_one = add_norm(own + nn(full_ctx, wout_v[...]) + row(0))
    hidden = normed_one * row(1) + row(2)
    hidden_low = hidden.astype(bf)
    run_beside(111)
    for k in range(4):
        cols = slice(768 * k, 768 * k + 768)
        if k % 2 == 0:
            arrive(1 + k // 2)
        flatten(wup_g, wup_v, cols)
        raised = nn(hidden_low, wup_v[:, cols]) + row(6 + k)
        normal = 0.5 + 0.5 * lax.erf(raised * (0.5**0.5))
        active[:, cols] = (raised * normal).astype(bf)
        slope[:, cols] = normal + raised * jnp.exp(-0.5 * raised * raised) * (0.5 / math.pi) ** 0.5
    run_beside(112)
    for n in (3, 4):
        arrive(n)
    branch = nn(active[...], wdown_g[...].reshape(3072, 768)) + row(3)
    normed_two, inv_two = add_norm(hidden + branch)
    lo[...] = (normed_two * row(4) + row(5)).astype(bf).reshape(2, 128, 768)
    for k in range(2):

        @pl.when(pi == k)
        def _():
            pltpu.make_async_copy(lo.at[k], lo_out.at[pi], lo_rs.at[pi]).start()

        @pl.when(pi != k)
        def _():
            remote(lo.at[k], lo_out.at[pi], lo_ss, lo_rs.at[pi], to_z).start()

    grad = cot_in[...].reshape(256, 768).astype(f32)
    gvec[4:5, :] = column_sum(grad * normed_two)
    gvec[5:6, :] = column_sum(grad)
    grad_second = norm_pull(grad * row(4), normed_two, inv_two)
    grad_branch = grad_second.astype(bf)
    gvec[3:4, :] = column_sum(grad_branch.astype(f32))

    def halves(n, full, back, rows, part):
        def at(xs, ys, core):
            start = (xs * 16 + (ys * 2 + core) * 4) * (rows // 4)
            return pl.ds(pl.multiple_of(start, rows // 4 * 4), rows)

        for xs in range(2):
            for ys in range(2):
                remote(
                    full.at[at(xs, ys, 1 - c), part],
                    back.at[xs, ys, :, part],
                    c_ss.at[n, xs, ys],
                    c_rs.at[n, xs, ys],
                    to_c,
                ).start()

    def settle(full, back, rows, out, sems, base, parts):
        for xs in range(2):
            for ys in range(2):
                for n, part in parts:
                    wait_for(back.at[xs, ys, :, part], c_rs.at[n, xs, ys])

                def body(t, carry):
                    rel = pl.multiple_of(t * 16, 16)
                    start = (xs * 16 + (ys * 2 + c) * 4) * (rows // 4)
                    mine = full[pl.ds(pl.multiple_of(start + rel, 16), 16), :].astype(f32)
                    there = pl.ds(rel, 16)
                    back[xs, ys, there, :] = (
                        mine + back[xs, ys, there, :].astype(f32)
                    ).astype(bf)
                    return carry

                lax.fori_loop(0, rows // 16, body, 0)
                if out is not None:
                    k = base + xs * 2 + ys
                    pltpu.make_async_copy(back.at[xs, ys], out.at[xs, ys], sems.at[k]).start()

    def spread_down():
        settle(gd, rd, 384, None, o_sem, 0, [(0, pl.ds(0, 768))])
        for k in range(2):
            remote(
                rd.at[k, 1 - y, pl.ds(0, 192)], r2a.at[k], s2_ss.at[k], s2_rs.at[k], to_y
            ).start()
            remote(
                rd.at[1 - x, k, pl.ds(192, 192)], r2b.at[k], s2_ss.at[2 + k], s2_rs.at[2 + k], to_x
            ).start()

    def collect_down():
        for k in range(2):
            wait_for(r2a.at[k], s2_rs.at[k])
            wait_for(r2b.at[k], s2_rs.at[2 + k])

        def body(t, carry):
            k, rel = lax.div(t, 12), pl.multiple_of(lax.rem(t, 12) * 16, 16)
            a, b = pl.ds(rel, 16), pl.ds(pl.multiple_of(rel + 192, 16), 16)
            rd[k, y, a, :] = (rd[k, y, a, :].astype(f32) + r2a[k, a, :].astype(f32)).astype(bf)
            rd[x, k, b, :] = (rd[x, k, b, :].astype(f32) + r2b[k, a, :].astype(f32)).astype(bf)
            return carry

        lax.fori_loop(0, 24, body, 0)
        for k in range(2):
            wait_for(r2a.at[k], s2_ss.at[k])
            wait_for(r2b.at[k], s2_ss.at[2 + k])
        for k in range(4):
            xs, ys = k // 2, k % 2
            pltpu.make_async_copy(rd.at[xs, ys], gdown_h.at[xs, ys], o_sem.at[k]).start()

    for k in range(4):
        rows = slice(768 * k, 768 * k + 768)
        gd[rows, :] = tn(active[:, rows], grad_branch).astype(bf)
    halves(0, gd, rd, 384, pl.ds(0, 768))
    for k in range(4):
        cols = slice(768 * k, 768 * k + 768)
        pulled = (nt(grad_branch, wdown_g[8 * k : 8 * k + 8].reshape(768, 768)) * slope[:, cols]).astype(bf)
        active[:, cols] = pulled
        gvec[6 + k : 7 + k, :] = column_sum(pulled.astype(f32))
        gu[:, cols] = tn(hidden_low, pulled).astype(bf)
        halves(1 + k, gu, ru, 96, pl.ds(768 * k, 768))
        if k == 1:
            spread_down()
    grad_hidden = grad_second + nt(active[...], wup_v[...])
    gvec[1:2, :] = column_sum(grad_hidden * normed_one)
    gvec[2:3, :] = column_sum(grad_hidden)
    grad_first = norm_pull(grad_hidden * row(1), normed_one, inv_one)
    dr1[...] = grad_first.reshape(2, 128, 768)
    grad_attended = grad_first.astype(bf)
    gvec[0:1, :] = column_sum(grad_attended.astype(f32))
    gvec[10:16, :] = jnp.zeros((6, 768), f32)
    go[...] = tn(full_ctx, grad_attended).astype(bf)
    halves(5, go, ro, 96, pl.ds(0, 768))
    back = nt(grad_attended, wout_v[...]).astype(bf)
    for q in range(4):
        dctx[q] = back[:, 192 * q : 192 * q + 192].reshape(2, 128, 192)

    for t in range(2):
        j = (2 * t + zl) * 2 + y
        for k, (dev, target) in enumerate(
            ((to_n, 2 * (1 - zl) + y), (to_y, 2 * zl + 1 - y), (to_d, 2 * (1 - zl) + 1 - y))
        ):
            remote(dctx.at[target, t], dc_all.at[j], dc_ss.at[t, k], dc_rs.at[j], dev).start()
        pltpu.make_async_copy(dctx.at[g, t], dc_all.at[j], dc_rs.at[j]).start()

    settle(gu, ru, 96, gup_h, o_sem, 4, [(1 + k, pl.ds(768 * k, 768)) for k in range(4)])
    settle(go, ro, 96, gout_h, o_sem, 8, [(5, pl.ds(0, 768))])
    collect_down()
    for k in range(2):
        wait_for(lo_out.at[k], lo_rs.at[k])
        for n in range(3):
            wait_for(dctx.at[0, 0], dc_ss.at[k, n])
    wait_for(lo.at[0], lo_ss)
    for k in range(8):
        wait_for(dc_all.at[k], dc_rs.at[k])
    for n in range(6):
        for xs in range(2):
            for ys in range(2):
                gone = gd.at[pl.ds(0, 384)] if n == 0 else gu.at[pl.ds(0, 96), pl.ds(0, 768)]
                wait_for(gone, c_ss.at[n, xs, ys])
    for first, out in ((0, gdown_h), (4, gup_h), (8, gout_h)):
        for k in range(4):
            wait_for(out.at[k // 2, k % 2], o_sem.at[first + k])

    wait_for(cot.at[0], cot_ss)
    for i in range(2):
        for q in range(SUB):
            wait_for(tok.at[0, cuts[q]], tz_ss.at[i, q])
    for k in range(2, 4):

        @pl.when(inner)
        def _():
            for q in range(SUB):
                wait_for(tok.at[0, cuts[q]], tx_ss.at[k, q])

    for k in range(4):
        for q in range(SUB):
            wait_for(tok.at[0, cuts[q]], ty_ss.at[k, q])
    for k in range(8):
        wait_for(tok.at[0], tc_ss.at[k])
    for k in range(3):
        wait_for(wq.at[0], wq_ss.at[k])
    for k in range(3, 10):
        wait_for(land.at[0, 0, 0], wq_ss.at[k])
    for n in range(count):
        for k in range(2):
            wait_for(shard(n), wz_ss.at[n, k])

        @pl.when(inner)
        def _():
            wait_for(two(n), wz_ss.at[n, 2])

    for n, k in sent:
        gone = some(n, k - 3) if k in (3, 4) else at(n, quad(0, 0))
        wait_for(gone, wp_ss.at[n, k])
    for j in range(8):
        zz, yy = j // 2, j % 2
        stay = jnp.logical_and(zl == zz % 2, y == yy)

        @pl.when(jnp.logical_not(stay))
        def _():
            wait_for(ctx.at[j], ctx_ss.at[j])

    for k, (src, dst) in enumerate(kept):
        wait_for(dst, out_sem.at[k])


def forward_call(tokens, cot, segments, wqkv, wout, wup, wdown, rows24, up_bias, qv_bias):
    bf, f32 = jnp.bfloat16, jnp.float32
    sds = jax.ShapeDtypeStruct
    dma = pltpu.SemaphoreType.DMA
    outs = [
        sds((2, 128, 768), f32),
        sds((16, 768), f32),
        sds((2, 128, 768), bf),
        sds((8, 128, 192), bf),
        sds((2, 2, 96, 768), bf),
        sds((2, 2, 96, 3072), bf),
        sds((2, 2, 384, 768), bf),
        sds((16, 128, 768), bf),
        sds((3, 1024, 64), bf),
        sds((3, 2048, 64), bf),
        sds((3, 2048, 64), bf),
        sds((3, 1024, 64), f32),
        sds((3, 8, 1024), f32),
        sds((768, 576), bf),
        sds((8, 2048), f32),
        sds((2048, 128), f32),
    ]
    scratch = [
        pltpu.VMEM((16, 128, 768), bf),
        pltpu.VMEM((2, 2, 2, 4, 32, 576), bf),
        pltpu.VMEM((768, 576), bf),
        pltpu.VMEM((3, 1024, 64), bf),
        pltpu.VMEM((3, 2048, 64), bf),
        pltpu.VMEM((3, 2048, 64), bf),
        pltpu.VMEM((3, 1024, 64), f32),
        pltpu.VMEM((3, 8, 1024), f32),
        pltpu.VMEM((8, 2048), f32),
        pltpu.VMEM((2048, 128), f32),
        pltpu.VMEM((8, 128, 192), bf),
        pltpu.VMEM((32, 24, 768), bf),
        pltpu.VMEM((32, 24, 3072), bf),
        pltpu.VMEM((32, 96, 768), bf),
        pltpu.VMEM((8, 8, 576), f32),
        pltpu.VMEM((4, 2, 128, 192), bf),
        pltpu.VMEM((2, 128, 768), bf),
        pltpu.VMEM((768, 768), bf),
        pltpu.VMEM((768, 3072), bf),
        pltpu.VMEM((256, 3072), bf),
        pltpu.VMEM((256, 3072), f32),
        pltpu.VMEM((768, 768), bf),
        pltpu.VMEM((768, 3072), bf),
        pltpu.VMEM((3072, 768), bf),
        pltpu.VMEM((2, 2, 96, 768), bf),
        pltpu.VMEM((2, 2, 96, 3072), bf),
        pltpu.VMEM((2, 2, 384, 768), bf),
        dma((16, SUB)),
        dma((2, SUB)),
        dma((4, SUB)),
        dma((4, SUB)),
        dma((8,)),
        dma(()),
        dma((2,)),
        dma((10,)),
        dma((2, 2, 2, 4)),
        dma((len(PIECES), 3)),
        dma((len(PIECES), 5)),
        dma((len(PIECES), 8)),
        dma((len(PIECES), 2, 4, 2)),
        dma((8,)),
        dma((4, 2)),
        dma((9,)),
        dma((6, 2, 2)),
        dma((6, 2, 2)),
        dma((12,)),
        pltpu.VMEM((4, 32, 576), bf),
        pltpu.VMEM((2, 128, 768), bf),
        pltpu.VMEM((4, 2, 128, 192), bf),
        pltpu.VMEM((2, 192, 768), bf),
        pltpu.VMEM((2, 192, 768), bf),
        dma(()),
        dma((2,)),
        dma((2, 3)),
        dma((8,)),
        dma((4,)),
        dma((4,)),
    ]
    here, far = pl.BlockSpec(memory_space=pltpu.VMEM), pl.BlockSpec(memory_space=ANY)
    return pl.pallas_call(
        forward_kernel,
        out_shape=outs,
        in_specs=[far, far, here, here, far, far, far, here, here, here],
        out_specs=[here] * 2 + [far] * (len(outs) - 2),
        scratch_shapes=scratch,
        compiler_params=pltpu.CompilerParams(
            collective_id=0, has_side_effects=True, vmem_limit_bytes=VMEM_LIMIT
        ),
        name="forward",
    )(tokens, cot, segments, wqkv, wout, wup, wdown, rows24, up_bias, qv_bias)


RCUT = 2
EARLY_JOBS = 2
JOBS = (
    ("down", (48, 768), 0, 0),
    ("down", (48, 768), 48, 0),
    ("up", (24, 1536), 0, 0),
    ("up", (24, 1536), 0, 1536),
    ("out", (24, 768), 0, 0),
)


def add_block(dst, src):
    dst[...] = (dst[...].astype(jnp.float32) + src[...].astype(jnp.float32)).astype(jnp.bfloat16)


def backward_kernel(
    dc_h,
    dr1,
    gout,
    gup,
    gdown,
    gvec,
    tok_h,
    q_h,
    k_h,
    v_h,
    o_h,
    lse_h,
    wq_h,
    idrow_h,
    idcol_h,
    gt_out,
    gout_o,
    gup_o,
    gdown_o,
    gq_o,
    small_o,
    *rest,
):
    count = len(JOBS)
    accs, rest = rest[:count], rest[count:]
    r2as, rest = rest[:count], rest[count:]
    r2bs, rest = rest[:count], rest[count:]
    r1as, rest = rest[:count], rest[count:]
    r1bs, rest = rest[:count], rest[count:]
    rzs, rest = rest[:count], rest[count:]
    (
        tok,
        qs,
        ks,
        vs,
        os_,
        lses,
        wqs,
        idrow,
        idcol,
        dc,
        dks,
        dvs,
        dqs,
        douts,
        kv_send,
        kv_recv,
        dmix,
        dx,
        rx,
        dr,
        gt_send,
        gt_in,
        gq,
        gqc,
        gqx,
        gqz,
        gqin,
        gva,
        gvr,
        qb,
        qbr,
        qb_o,
        in_sem,
        own_ss,
        s2_ss,
        s2_rs,
        s1_ss,
        s1_rs,
        z_ss,
        z_rs,
        kv_ss,
        kv_rs,
        dx_ss,
        dx_rs,
        gt_ss,
        gt_rs,
        gq_ss,
        gq_rs,
        gv_ss,
        gv_rs,
        qb_ss,
        qb_rs,
    ) = rest
    x, y, c, h, z = place()
    zl, pi = lax.rem(z, 2), lax.div(z, 2)
    pz, zc = z + 1 - 2 * zl, lax.rem(z + 2, 4)
    g = 2 * zl + y
    hy = lax.rem(h + 2, 4)
    hc = h + 1 - 2 * c
    to_x, to_y, to_c = (1 - x, h, z), (x, hy, z), (x, hc, z)
    to_n, to_d, to_z = (x, h, pz), (x, hy, pz), (x, h, zc)
    sources = {"out": gout, "up": gup, "down": gdown}
    greet(peers_of(x, h, c, z))

    def loaded():
        return (
            (tok_h, tok),
            (q_h, qs),
            (k_h, ks),
            (v_h, vs),
            (o_h, os_),
            (lse_h, lses),
            (wq_h, wqs),
            (idrow_h, idrow),
            (idcol_h, idcol),
            (dr1, dr),
            (gvec, gva),
            (dc_h, dc),
        )

    for k, (src, dst) in enumerate(loaded()):
        pltpu.make_async_copy(src, dst, in_sem.at[k]).start()
    def part_of(n):
        name, shape, row, col = JOBS[n]
        return sources[name], (pl.ds(row, shape[0]), pl.ds(col, shape[1]))

    def cross(n, source, part):
        remote(
            source.at[(1 - x, y, pl.ds(0, RCUT)) + part],
            r1as[n],
            s1_ss.at[n, 0],
            s1_rs.at[n, 0],
            to_x,
        ).start()
        remote(
            source.at[(x, 1 - y, pl.ds(RCUT, 4 - RCUT)) + part],
            r1bs[n],
            s1_ss.at[n, 1],
            s1_rs.at[n, 1],
            to_y,
        ).start()

    def stage1(n):
        src, part = part_of(n)
        acc = accs[n]
        if n < EARLY_JOBS:
            cross(n, src, part)
            pltpu.make_async_copy(
                src.at[(x, y, pl.ds(0, 4)) + part], acc.at[x, y], own_ss.at[n, 0]
            ).start()
            return
        for k in range(2):
            remote(
                src.at[(k, 1 - y, pl.ds(0, RCUT)) + part],
                r2as[n].at[k],
                s2_ss.at[n, k],
                s2_rs.at[n, k],
                to_y,
            ).start()
            remote(
                src.at[(1 - x, k, pl.ds(RCUT, 4 - RCUT)) + part],
                r2bs[n].at[k],
                s2_ss.at[n, 2 + k],
                s2_rs.at[n, 2 + k],
                to_x,
            ).start()
        for k in range(2):
            pltpu.make_async_copy(
                src.at[(k, y, pl.ds(0, RCUT)) + part], acc.at[k, y, pl.ds(0, RCUT)], own_ss.at[n, k]
            ).start()
            pltpu.make_async_copy(
                src.at[(x, k, pl.ds(RCUT, 4 - RCUT)) + part],
                acc.at[x, k, pl.ds(RCUT, 4 - RCUT)],
                own_ss.at[n, 2 + k],
            ).start()

    for n in range(count):
        stage1(n)
    def stage2(n):
        acc = accs[n]
        if n < EARLY_JOBS:
            wait_for(acc.at[x, y], own_ss.at[n, 0])
            return
        for k in range(2):
            wait_for(r2as[n].at[k], s2_rs.at[n, k])
            wait_for(r2bs[n].at[k], s2_rs.at[n, 2 + k])
            wait_for(r2as[n].at[k], own_ss.at[n, k])
            wait_for(r2bs[n].at[k], own_ss.at[n, 2 + k])
        for k in range(2):
            for q in range(RCUT):
                add_block(acc.at[k, y, q], r2as[n].at[k, q])
            for q in range(4 - RCUT):
                add_block(acc.at[x, k, RCUT + q], r2bs[n].at[k, q])
        cross(n, acc, ())

    def stage3(n):
        acc = accs[n]
        wait_for(r1as[n], s1_rs.at[n, 0])
        wait_for(r1bs[n], s1_rs.at[n, 1])
        for q in range(RCUT):
            add_block(acc.at[x, y, q], r1as[n].at[q])
        for q in range(4 - RCUT):
            add_block(acc.at[x, y, RCUT + q], r1bs[n].at[q])
        for k in range(1, 4):
            zz = lax.rem(z + k, 4)
            remote(
                acc.at[x, y, zz], rzs[n].at[z], z_ss.at[n, k - 1], z_rs.at[n, z], (x, h, zz)
            ).start()

    def stage4(n):
        acc = accs[n]
        name, shape, row, col = JOBS[n]
        total = acc[x, y, z].astype(jnp.float32)
        for k in range(1, 4):
            zz = lax.rem(z + k, 4)
            wait_for(rzs[n].at[zz], z_rs.at[n, zz])
            total = total + rzs[n][zz].astype(jnp.float32)
        out = {"out": gout_o, "up": gup_o, "down": gdown_o}[name]
        out[row : row + shape[0], col : col + shape[1]] = total

    for k, (src, dst) in enumerate(loaded()):
        wait_for(dst, in_sem.at[k])

    def attend(zz):
        rows = slice(zz * 256, zz * 256 + 256)
        first = pl.ds(pl.multiple_of((zz * 4 + c) * 128, 128), 128)
        second = pl.ds(pl.multiple_of((zz * 4 + 2 + c) * 128, 128), 128)
        idq = jnp.concatenate([idrow[0:1, first], idrow[0:1, second]], axis=1)
        mask = idcol[:, 0:1] == idq
        both = jnp.concatenate([dc[2 * zz], dc[2 * zz + 1]], axis=0)
        for hh in range(3):
            douts[hh] = both[:, 64 * hh : 64 * hh + 64]

        def one_head(hh, carry):
            dout = douts[hh]
            q = qs[hh, rows, :]
            delta = jnp.sum(dout.astype(jnp.float32) * os_[hh, rows, :], axis=-1, keepdims=True)
            delta = jnp.transpose(jnp.broadcast_to(delta, (256, 128)))[0:1, :]
            scores = jnp.where(mask, nt(ks[hh], q), MASKED)
            probs = jnp.exp(scores - lses[hh, 0:1, rows])
            dprobs = nt(vs[hh], dout)
            ds = (probs * (dprobs - delta)).astype(jnp.bfloat16)
            dk = nn(ds, q)
            dv = nn(probs.astype(jnp.bfloat16), dout)
            if zz == 0:
                dks[hh] = dk
                dvs[hh] = dv
            else:
                dks[hh] += dk
                dvs[hh] += dv
            dqs[hh, rows, :] = (tn(ds, ks[hh]) * SCALE).astype(jnp.bfloat16)
            return carry

        lax.fori_loop(0, 3, one_head, 0)

    def add_gv(k):
        wait_for(gva, gv_rs.at[k])
        wait_for(gva, gv_ss.at[k])
        gva[...] = gva[...] + gvr[k]

    def gv_stage(n):
        if n < 3:
            if n > 0:
                add_gv(n - 1)
            remote(gva, gvr.at[n], gv_ss.at[n], gv_rs.at[n], (to_c, to_x, to_y)[n]).start()
        elif n == 3:
            add_gv(2)
            for k in range(1, 4):
                remote(
                    gva,
                    gvr.at[3 + z],
                    gv_ss.at[2 + k],
                    gv_rs.at[3 + z],
                    (x, h, lax.rem(z + k, 4)),
                ).start()
        else:
            gv = gva[...]
            for k in range(1, 4):
                zz = lax.rem(z + k, 4)
                wait_for(gvr.at[3 + zz], gv_rs.at[3 + zz])
                gv = gv + gvr[3 + zz]
            gvr[3 + z] = gv

    gv_stage(0)
    beside = {
        0: ((stage2, 0), (stage3, 0), (stage2, 1), (stage3, 1)),
        1: ((stage2, 2),),
        2: ((stage2, 3), (stage3, 2)),
    }
    for t in range(4):
        attend(t)
        gv_stage(t + 1)
        for stage, n in beside.get(t, ()):
            stage(n)

    for j in range(8):
        p = (j // 2) * 4 + (j % 2) * 2 + 1 - c
        rows = pl.ds(pl.multiple_of(p * 128, 128), 128)
        kv_send[j] = jnp.concatenate(
            [dks[hh, rows, :] for hh in range(3)] + [dvs[hh, rows, :] for hh in range(3)], axis=1
        ).astype(jnp.bfloat16)
    remote(kv_send, kv_recv, kv_ss, kv_rs, to_c).start()
    stage2(4)
    stage3(3)
    wait_for(kv_recv, kv_rs)

    qsum = jnp.zeros((1, 192), jnp.float32)
    vsum = jnp.zeros((1, 192), jnp.float32)
    for j in range(8):
        p = (j // 2) * 4 + (j % 2) * 2 + c
        rows = pl.ds(pl.multiple_of(p * 128, 128), 128)
        wide = jnp.concatenate(
            [dks[hh, rows, :] for hh in range(3)] + [dvs[hh, rows, :] for hh in range(3)], axis=1
        )
        wide = (wide + kv_recv[j].astype(jnp.float32)).astype(jnp.bfloat16)
        part = jnp.concatenate([dqs[hh, 128 * j : 128 * j + 128, :] for hh in range(3)], axis=1)
        dmix[128 * j : 128 * j + 128, :] = jnp.concatenate([part, wide], axis=1)
        qsum = qsum + jnp.sum(part.astype(jnp.float32), axis=0, keepdims=True)
        vsum = vsum + jnp.sum(wide[:, 192:].astype(jnp.float32), axis=0, keepdims=True)
    none = jnp.zeros((1, 192), jnp.float32)
    qb[...] = jnp.broadcast_to(
        jnp.concatenate([qsum, none, vsum, none[:, :64]], axis=1), (8, 640)
    )
    remote(qb, qbr.at[0], qb_ss.at[0], qb_rs.at[0], to_c).start()

    for j in range(8):
        zz, yy = j // 2, j % 2
        dx[j] = nt(dmix[128 * j : 128 * j + 128, :], wqs[...]).astype(jnp.bfloat16)
        slot = zz // 2
        stay = jnp.logical_and(zl == zz % 2, y == yy)

        @pl.when(jnp.logical_not(stay))
        def _():
            remote(
                dx.at[j],
                rx.at[g, slot],
                dx_ss.at[j],
                dx_rs.at[g, slot],
                (x, yy * 2 + c, 2 * pi + zz % 2),
            ).start()

        @pl.when(stay)
        def _():
            pltpu.make_async_copy(dx.at[j], rx.at[g, slot], dx_rs.at[g, slot]).start()

    total = jnp.zeros((768, 576), jnp.float32)
    for zz in range(4):
        left = jnp.concatenate([tok[zz * 4 + c], tok[zz * 4 + 2 + c]], axis=0)
        total = total + tn(left, dmix[256 * zz : 256 * zz + 256, :])
    for xs in range(2):
        for hs in range(4):
            for zz in range(4):
                base = (xs * 16 + hs * 4 + zz) * 24
                gq[hs % 2, xs, zz // 2, 2 * (zz % 2) + hs // 2] = total[base : base + 24].astype(jnp.bfloat16)
    remote(gq.at[1 - c], gqc, gq_ss.at[0], gq_rs.at[0], to_c).start()
    stage3(4)
    stage4(0)

    def add_qb(k):
        wait_for(qb, qb_rs.at[k])
        wait_for(qb, qb_ss.at[k])
        qb[...] = qb[...] + qbr[k]

    wait_for(gqc, gq_rs.at[0])

    def addq(t, carry):
        i, q = lax.div(t, 4), lax.rem(t, 4)
        xs, pp = lax.div(i, 2), lax.rem(i, 2)
        add_block(gq.at[c, xs, pp, q], gqc.at[xs, pp, q])
        return carry

    lax.fori_loop(0, 16, addq, 0)
    remote(gq.at[c, 1 - x], gqx, gq_ss.at[1], gq_rs.at[1], to_x).start()
    add_qb(0)
    remote(qb, qbr.at[1], qb_ss.at[1], qb_rs.at[1], to_x).start()
    stage4(1)
    wait_for(gqx, gq_rs.at[1])

    def addx(t, carry):
        pp, q = lax.div(t, 4), lax.rem(t, 4)
        add_block(gq.at[c, x, pp, q], gqx.at[pp, q])
        return carry

    lax.fori_loop(0, 8, addx, 0)
    remote(gq.at[c, x, 1 - pi], gqz, gq_ss.at[2], gq_rs.at[2], to_z).start()
    add_qb(1)
    remote(qb, qbr.at[2], qb_ss.at[2], qb_rs.at[2], to_z).start()
    stage4(2)

    for s in range(2):
        acc = dr[s]
        for q in range(4):
            wait_for(rx.at[q, s], dx_rs.at[q, s])
            acc = acc + rx[q, s].astype(jnp.float32)
        gt_send[s] = acc.astype(jnp.bfloat16)
        zz = 2 * s + zl
        row = pi
        stay = pi == s

        @pl.when(stay)
        def _():
            pltpu.make_async_copy(gt_send.at[s], gt_in.at[row], gt_rs.at[row]).start()

        @pl.when(jnp.logical_not(stay))
        def _():
            remote(gt_send.at[s], gt_in.at[row], gt_ss.at[s], gt_rs.at[row], to_z).start()

    wait_for(gqz, gq_rs.at[2])
    for q in range(4):
        add_block(gq.at[c, x, pi, q], gqz.at[q])
    add_qb(2)
    gqzs = gq.at[c, x, pi]
    for k, (dev, target) in enumerate(
        ((to_n, 2 * (1 - zl) + y), (to_y, 2 * zl + 1 - y), (to_d, 2 * (1 - zl) + 1 - y))
    ):
        remote(gqzs.at[target], gqin.at[g], gq_ss.at[3 + k], gq_rs.at[3 + g], dev).start()
        remote(qb, qb_o.at[g], qb_ss.at[3 + k], qb_rs.at[3 + g], dev).start()
    pltpu.make_async_copy(gqzs.at[g], gqin.at[g], gq_rs.at[3 + g]).start()
    pltpu.make_async_copy(qb, qb_o.at[g], qb_rs.at[3 + g]).start()
    stage4(3)
    for q in range(4):
        wait_for(gqin.at[q], gq_rs.at[3 + q])
        wait_for(qb_o.at[q], qb_rs.at[3 + q])
        gq_o[q] = gqin[q].astype(jnp.float32)
    me = x * 16 + h * 4 + z
    vectors = gvr[3 + z]
    own_rows = pltpu.roll(vectors[0:8, :], lax.rem(768 - 24 * me, 768), 1)[:, 0:128]
    up_row = jnp.zeros((1, 768), jnp.float32)
    for i in range(4):
        up_row = up_row + jnp.where(lax.div(me, 8) == i, vectors[6 + i : 7 + i, :], 0.0)
    up_rows = jnp.broadcast_to(up_row, (8, 768))
    up_rows = pltpu.roll(up_rows, lax.rem(768 - 96 * lax.rem(me, 8), 768), 1)[:, 0:128]
    qv_rows = pltpu.roll(qb_o[h], lax.rem(640 - 48 * z - 384 * x, 640), 1)[:, 0:128]
    line = lax.broadcasted_iota(jnp.int32, (8, 128), 0)
    small_o[...] = jnp.where(line < 6, own_rows, jnp.where(line == 6, up_rows, qv_rows))
    stage4(4)
    for i in range(2):
        wait_for(gt_in.at[i], gt_rs.at[i])
        gt_out[i] = gt_in[i].astype(jnp.float32)

    for s in range(2):

        @pl.when(pi != s)
        def _():
            wait_for(gt_send.at[s], gt_ss.at[s])

    for n in range(count):
        for k in range(2 if n >= EARLY_JOBS else 0):
            wait_for(r1as[n], s2_ss.at[n, k])
            wait_for(r1bs[n], s2_ss.at[n, 2 + k])
        wait_for(r1as[n], s1_ss.at[n, 0])
        wait_for(r1bs[n], s1_ss.at[n, 1])
        for k in range(3):
            wait_for(rzs[n].at[0], z_ss.at[n, k])
    wait_for(kv_send, kv_ss)
    for j in range(8):
        stay = jnp.logical_and(zl == (j // 2) % 2, y == j % 2)

        @pl.when(jnp.logical_not(stay))
        def _():
            wait_for(dx.at[j], dx_ss.at[j])

    wait_for(gqc, gq_ss.at[0])
    wait_for(gqx, gq_ss.at[1])
    wait_for(gqz, gq_ss.at[2])
    for k in range(3):
        wait_for(gqin.at[0], gq_ss.at[3 + k])
        wait_for(qb, qb_ss.at[3 + k])
        wait_for(gva, gv_ss.at[3 + k])


def backward_call(*args):
    bf, f32 = jnp.bfloat16, jnp.float32
    sds = jax.ShapeDtypeStruct
    dma = pltpu.SemaphoreType.DMA
    vm = pltpu.VMEM
    outs = [
        sds((2, 128, 768), f32),
        sds((24, 768), f32),
        sds((24, 3072), f32),
        sds((96, 768), f32),
        sds((4, 24, 576), f32),
        sds((8, 128), f32),
    ]
    shapes = [job[1] for job in JOBS]
    count = len(JOBS)
    scratch = (
        [vm((2, 2, 4) + s, bf) for s in shapes]
        + [vm((2, RCUT) + s, bf) for s in shapes]
        + [vm((2, 4 - RCUT) + s, bf) for s in shapes]
        + [vm((RCUT,) + s, bf) for s in shapes]
        + [vm((4 - RCUT,) + s, bf) for s in shapes]
        + [vm((4,) + s, bf) for s in shapes]
        + [
            vm((16, 128, 768), bf),
            vm((3, 1024, 64), bf),
            vm((3, 2048, 64), bf),
            vm((3, 2048, 64), bf),
            vm((3, 1024, 64), f32),
            vm((3, 8, 1024), f32),
            vm((768, 576), bf),
            vm((8, 2048), f32),
            vm((2048, 128), f32),
            vm((8, 128, 192), bf),
            vm((3, 2048, 64), f32),
            vm((3, 2048, 64), f32),
            vm((3, 1024, 64), bf),
            vm((3, 256, 64), bf),
            vm((8, 128, 384), bf),
            vm((8, 128, 384), bf),
            vm((1024, 576), bf),
            vm((8, 128, 768), bf),
            vm((4, 2, 128, 768), bf),
            vm((2, 128, 768), f32),
            vm((2, 128, 768), bf),
            vm((2, 128, 768), bf),
            vm((2, 2, 2, 4, 24, 576), bf),
            vm((2, 2, 4, 24, 576), bf),
            vm((2, 4, 24, 576), bf),
            vm((4, 24, 576), bf),
            vm((4, 24, 576), bf),
            vm((16, 768), f32),
            vm((7, 16, 768), f32),
            vm((8, 640), f32),
            vm((3, 8, 640), f32),
            vm((4, 8, 640), f32),
            dma((12,)),
            dma((count, 4)),
            dma((count, 4)),
            dma((count, 4)),
            dma((count, 2)),
            dma((count, 2)),
            dma((count, 3)),
            dma((count, 4)),
            dma(()),
            dma(()),
            dma((8,)),
            dma((4, 2)),
            dma((2,)),
            dma((2,)),
            dma((6,)),
            dma((7,)),
            dma((6,)),
            dma((7,)),
            dma((6,)),
            dma((7,)),
        ]
    )
    here = pl.BlockSpec(memory_space=pltpu.VMEM)
    far = pl.BlockSpec(memory_space=ANY)
    return pl.pallas_call(
        backward_kernel,
        out_shape=outs,
        in_specs=[far] * 15,
        out_specs=[here] * 6,
        scratch_shapes=scratch,
        compiler_params=pltpu.CompilerParams(
            collective_id=1, has_side_effects=True, vmem_limit_bytes=VMEM_LIMIT
        ),
        name="backward",
    )(*args)


def finish_kernel(lo, gt, gq, gout, gup, gdown, small, lo_o, gt_o, gqkv_o, gout_o, gup_o, gdown_o, *vectors):
    for src, dst in ((lo, lo_o), (gt, gt_o), (gout, gout_o), (gup, gup_o), (gdown, gdown_o)):
        dst[...] = src[...]
    for part in range(3):
        gqkv_o[:, 768 * part : 768 * part + 768] = jnp.concatenate(
            [gq[q, :, 192 * part : 192 * part + 192] for q in range(4)], axis=1
        )
    for k, dst in enumerate(vectors):
        dst[...] = small[k : k + 1, : dst.shape[1]]


def finish_call(lo, gt, gq, gout, gup, gdown, small):
    f32 = jnp.float32
    here = pl.BlockSpec(memory_space=pltpu.VMEM)
    like = lambda a: jax.ShapeDtypeStruct(a.shape, a.dtype)
    wide = jax.ShapeDtypeStruct((24, 2304), f32)
    outs = [like(lo), like(gt), wide, like(gout), like(gup), like(gdown)]
    outs += [jax.ShapeDtypeStruct((1, width), f32) for width in (24,) * 6 + (96, 48)]
    return pl.pallas_call(
        finish_kernel,
        out_shape=outs,
        in_specs=[here] * 7,
        out_specs=[here] * len(outs),
        compiler_params=pltpu.CompilerParams(vmem_limit_bytes=VMEM_LIMIT),
        name="finish",
    )(lo, gt, gq, gout, gup, gdown, small)


def slab_body(
    tokens,
    segments,
    qkv_weight,
    qv_bias,
    out_weight,
    out_bias,
    attn_gain,
    attn_shift,
    up_weight,
    up_bias,
    down_weight,
    down_bias,
    ffn_gain,
    ffn_shift,
    cotangent,
):
    rows24 = jnp.stack([out_bias, attn_gain, attn_shift, down_bias, ffn_gain, ffn_shift])
    (
        grad_first,
        gvec,
        lo_out,
        dc_all,
        grad_out,
        grad_up,
        grad_down,
        tok_all,
        q_all,
        k_all,
        v_all,
        o_all,
        lse_all,
        wq_all,
        idrow_all,
        idcol_all,
    ) = forward_call(
        tokens,
        cotangent,
        segments,
        qkv_weight,
        out_weight,
        up_weight,
        down_weight,
        rows24,
        up_bias.reshape(1, 96),
        qv_bias.reshape(1, 48),
    )
    gt_out, gout_o, gup_o, gdown_o, gq_o, small = backward_call(
        dc_all,
        grad_first,
        grad_out.reshape(2, 2, 4, 24, 768),
        grad_up.reshape(2, 2, 4, 24, 3072),
        grad_down.reshape(2, 2, 4, 96, 768),
        gvec,
        tok_all,
        q_all,
        k_all,
        v_all,
        o_all,
        lse_all,
        wq_all,
        idrow_all,
        idcol_all,
    )
    lo_out, gt_out, gqkv, gout_o, gup_o, gdown_o, *vectors = finish_call(
        lo_out, gt_out, gq_o, gout_o, gup_o, gdown_o, small
    )
    rows = [vector.reshape(vector.shape[1]) for vector in vectors]
    return (
        lo_out,
        gt_out,
        gqkv,
        rows[7],
        gout_o,
        rows[0],
        rows[1],
        rows[2],
        gup_o,
        rows[6],
        gdown_o,
        rows[3],
        rows[4],
        rows[5],
    )


def solution(mesh):
    sizes = tuple(mesh.shape[name] for name in ("dp", "head", "blk"))
    body = slab_body if sizes == (2, 4, 4) else general_body
    placed = (
        P("dp", ("blk", "head"), None),
        P("dp", ("blk", "head")),
        P(("dp", "head", "blk"), None),
        P(("dp", "head", "blk")),
        P(("dp", "head", "blk"), None),
        P(("dp", "head", "blk")),
        P(("dp", "head", "blk")),
        P(("dp", "head", "blk")),
        P(("dp", "head", "blk"), None),
        P(("dp", "head", "blk")),
        P(("dp", "head", "blk"), None),
        P(("dp", "head", "blk")),
        P(("dp", "head", "blk")),
        P(("dp", "head", "blk")),
        P("dp", ("blk", "head"), None),
    )
    return jax.shard_map(
        body,
        mesh=mesh,
        in_specs=placed,
        out_specs=(
            P("dp", ("blk", "head"), None),
            P("dp", ("blk", "head"), None),
            P(("dp", "head", "blk"), None),
            P(("dp", "head", "blk")),
            P(("dp", "head", "blk"), None),
            P(("dp", "head", "blk")),
            P(("dp", "head", "blk")),
            P(("dp", "head", "blk")),
            P(("dp", "head", "blk"), None),
            P(("dp", "head", "blk")),
            P(("dp", "head", "blk"), None),
            P(("dp", "head", "blk")),
            P(("dp", "head", "blk")),
            P(("dp", "head", "blk")),
        ),
        check_vma=False,
    )
```

profile of v0, /device:TPU:11, one launch (start us, length us, event | category | flops | bytes accessed | tf_op | source)
XLA Modules:
  0.0 223.7 jit_solution(1529814993562086391)
XLA Ops:
  0.6 1.3 stack.27.rows24
  2.0 132.4 %forward.1 = (f32[2,128,768]{2,1,0:T(8,128)}, f32[16,768]{1,0:T(8,128)}, bf16[2,128,768]{2,1,0:T(8,128)(2,1)}, bf16[8,128,192]{2,1,0:T(8,128)(2,1)}, bf16[2,2,96...) custom-call(bf16[2,128,768]{2,1,0:T(8,128)(2,1)} %tokens.1, ...), custom_call_target="tpu_custom_call" | custom-call | tf_op jit(solution)/shard_map/forward/pallas_call | solution.py:1202
  134.4 86.2 %backward.1 = (f32[2,128,768]{2,1,0:T(8,128)}, f32[24,768]{1,0:T(8,128)}, f32[24,3072]{1,0:T(8,128)}, f32[96,768]{1,0:T(8,128)}, f32[4,24,576]{2,1,0:T(8,128)}, /*index=5*/f32[8,128]{1,0:T(8,128)}) custom-call(bf16[8,128,192]{2,1,0:T(8,128)(2,1)} %get-tuple-element.51.dc_h, f32[2,128,768]{2,1,0:T(8,128)} %get-tuple-element.52.dr1, ...), custom_call_target="tpu_custom_call" | custom-call | tf_op jit(solution)/shard_map/backward/pallas_call | solution.py:1772
  220.6 2.9 %finish.1 = (bf16[2,128,768]{2,1,0:T(8,128)(2,1)}, f32[2,128,768]{2,1,0:T(8,128)}, f32[24,2304]{1,0:T(8,128)}, f32[24,768]{1,0:T(8,128)}, f32[24,3072]{1,0:T(8,1...) custom-call(bf16[2,128,768]{2,1,0:T(8,128)(2,1)} %get-tuple-element., ...), custom_call_target="tpu_custom_call" | custom-call | tf_op jit(solution)/shard_map/finish/pallas_call | solution.py:1803
where the time goes:
time: 224 us
  Pallas kernels  221 us (99%)
    pallas_call x1, Pallas kernels, forward_call(): pl.pallas_call(forward_kernel, out_shape=outs, in_specs=[far, far, here,...  132 us
    pallas_call x1, Pallas kernels, backward_call(): pl.pallas_call(backward_kernel, out_shape=outs, in_specs=[far] * 15, out_...  86.2 us

commit v1 on v0

--- a/solution.py
+++ b/solution.py
@@ -436,18 +436,21 @@
     return jnp.sum(values_in, axis=0, keepdims=True)
 
 
-CUT = 1
+CUT = 2
 EARLY = 0
-AHEAD = 2
+AHEAD = 1
 BESIDE_TOKENS = {
-    99: ((0, 0), (0, 1)),
+    99: ((0, 0),),
     100: ((1, 0),),
-    101: ((1, 1), (1, 2)),
-    102: ((1, 3),),
-    104: ((1, 4),),
+    101: ((1, 1),),
+    102: ((1, 2),),
+    103: ((1, 3),),
+    105: ((1, 4),),
     111: ((1, 5),),
     112: ((1, 6),),
 }
+LATE = 1
+LATE_STEP = 7
 WQ_STEPS = (4, 5, 8)
 SUB = 2
 ROWS_SUB = 64
@@ -719,18 +722,8 @@
     give_slices(x, pi, 3, to_z)
     give_slices(x, pi, 4, to_x)
     give_slices(x, pi, 5, to_c)
-    for n in range(EARLY, count):
+    for n in range(EARLY, LATE):
         along_z(n)
-    for i in range(2):
-
-        @pl.when(pi == i)
-        def _():
-            pltpu.make_async_copy(cot.at[i], cot_in.at[pi], cot_rs.at[pi]).start()
-
-        @pl.when(pi != i)
-        def _():
-            remote(cot.at[i], cot_in.at[pi], cot_ss, cot_rs.at[pi], to_z).start()
-
     turns = (z, pz, zc, lax.rem(pz + 2, 4))
 
     def hand_on(p, q, sends, keep_sem):
@@ -774,9 +767,22 @@
         if t >= lag:
             side_piece(*order[t - lag])
         slices_step(t)
+        if t == LATE_STEP:
+            for n in range(LATE, count):
+                along_z(n)
         run_beside(t)
 
     run_beside(99)
+    for i in range(2):
+
+        @pl.when(pi == i)
+        def _():
+            pltpu.make_async_copy(cot.at[i], cot_in.at[pi], cot_rs.at[pi]).start()
+
+        @pl.when(pi != i)
+        def _():
+            remote(cot.at[i], cot_in.at[pi], cot_ss, cot_rs.at[pi], to_z).start()
+
     for k in range(4):
         zz = lax.rem(z + k, 4)
         for hh in (hc, lax.rem(hc + 2, 4)):
@@ -1212,15 +1218,18 @@
     )(tokens, cot, segments, wqkv, wout, wup, wdown, rows24, up_bias, qv_bias)
 
 
-RCUT = 2
-EARLY_JOBS = 2
+RCUT = 3
+EARLY_JOBS = 1
 JOBS = (
-    ("down", (48, 768), 0, 0),
-    ("down", (48, 768), 48, 0),
+    ("down", (96, 768), 0, 0),
     ("up", (24, 1536), 0, 0),
     ("up", (24, 1536), 0, 1536),
     ("out", (24, 768), 0, 0),
 )
+
+
+def cut_of(n):
+    return 2 if n < EARLY_JOBS else RCUT
 
 
 def add_block(dst, src):
@@ -1347,14 +1356,14 @@
 
     def cross(n, source, part):
         remote(
-            source.at[(1 - x, y, pl.ds(0, RCUT)) + part],
+            source.at[(1 - x, y, pl.ds(0, cut_of(n))) + part],
             r1as[n],
             s1_ss.at[n, 0],
             s1_rs.at[n, 0],
             to_x,
         ).start()
         remote(
-            source.at[(x, 1 - y, pl.ds(RCUT, 4 - RCUT)) + part],
+            source.at[(x, 1 - y, pl.ds(cut_of(n), 4 - cut_of(n))) + part],
             r1bs[n],
             s1_ss.at[n, 1],
             s1_rs.at[n, 1],
@@ -1418,10 +1427,10 @@
         acc = accs[n]
         wait_for(r1as[n], s1_rs.at[n, 0])
         wait_for(r1bs[n], s1_rs.at[n, 1])
-        for q in range(RCUT):
+        for q in range(cut_of(n)):
             add_block(acc.at[x, y, q], r1as[n].at[q])
-        for q in range(4 - RCUT):
-            add_block(acc.at[x, y, RCUT + q], r1bs[n].at[q])
+        for q in range(4 - cut_of(n)):
+            add_block(acc.at[x, y, cut_of(n) + q], r1bs[n].at[q])
         for k in range(1, 4):
             zz = lax.rem(z + k, 4)
             remote(
@@ -1504,9 +1513,9 @@
 
     gv_stage(0)
     beside = {
-        0: ((stage2, 0), (stage3, 0), (stage2, 1), (stage3, 1)),
-        1: ((stage2, 2),),
-        2: ((stage2, 3), (stage3, 2)),
+        0: ((stage2, 0), (stage3, 0)),
+        1: ((stage2, 1),),
+        2: ((stage2, 2), (stage3, 1)),
     }
     for t in range(4):
         attend(t)
@@ -1521,8 +1530,8 @@
             [dks[hh, rows, :] for hh in range(3)] + [dvs[hh, rows, :] for hh in range(3)], axis=1
         ).astype(jnp.bfloat16)
     remote(kv_send, kv_recv, kv_ss, kv_rs, to_c).start()
-    stage2(4)
-    stage3(3)
+    stage2(3)
+    stage3(2)
     wait_for(kv_recv, kv_rs)
 
     qsum = jnp.zeros((1, 192), jnp.float32)
@@ -1574,7 +1583,7 @@
                 base = (xs * 16 + hs * 4 + zz) * 24
                 gq[hs % 2, xs, zz // 2, 2 * (zz % 2) + hs // 2] = total[base : base + 24].astype(jnp.bfloat16)
     remote(gq.at[1 - c], gqc, gq_ss.at[0], gq_rs.at[0], to_c).start()
-    stage3(4)
+    stage3(3)
     stage4(0)
 
     def add_qb(k):
@@ -1594,7 +1603,6 @@
     remote(gq.at[c, 1 - x], gqx, gq_ss.at[1], gq_rs.at[1], to_x).start()
     add_qb(0)
     remote(qb, qbr.at[1], qb_ss.at[1], qb_rs.at[1], to_x).start()
-    stage4(1)
     wait_for(gqx, gq_rs.at[1])
 
     def addx(t, carry):
@@ -1606,7 +1614,7 @@
     remote(gq.at[c, x, 1 - pi], gqz, gq_ss.at[2], gq_rs.at[2], to_z).start()
     add_qb(1)
     remote(qb, qbr.at[2], qb_ss.at[2], qb_rs.at[2], to_z).start()
-    stage4(2)
+    stage4(1)
 
     for s in range(2):
         acc = dr[s]
@@ -1638,7 +1646,7 @@
         remote(qb, qb_o.at[g], qb_ss.at[3 + k], qb_rs.at[3 + g], dev).start()
     pltpu.make_async_copy(gqzs.at[g], gqin.at[g], gq_rs.at[3 + g]).start()
     pltpu.make_async_copy(qb, qb_o.at[g], qb_rs.at[3 + g]).start()
-    stage4(3)
+    stage4(2)
     for q in range(4):
         wait_for(gqin.at[q], gq_rs.at[3 + q])
         wait_for(qb_o.at[q], qb_rs.at[3 + q])
@@ -1654,7 +1662,7 @@
     qv_rows = pltpu.roll(qb_o[h], lax.rem(640 - 48 * z - 384 * x, 640), 1)[:, 0:128]
     line = lax.broadcasted_iota(jnp.int32, (8, 128), 0)
     small_o[...] = jnp.where(line < 6, own_rows, jnp.where(line == 6, up_rows, qv_rows))
-    stage4(4)
+    stage4(3)
     for i in range(2):
         wait_for(gt_in.at[i], gt_rs.at[i])
         gt_out[i] = gt_in[i].astype(jnp.float32)
@@ -1709,8 +1717,8 @@
         [vm((2, 2, 4) + s, bf) for s in shapes]
         + [vm((2, RCUT) + s, bf) for s in shapes]
         + [vm((2, 4 - RCUT) + s, bf) for s in shapes]
-        + [vm((RCUT,) + s, bf) for s in shapes]
-        + [vm((4 - RCUT,) + s, bf) for s in shapes]
+        + [vm((cut_of(n),) + s, bf) for n, s in enumerate(shapes)]
+        + [vm((4 - cut_of(n),) + s, bf) for n, s in enumerate(shapes)]
         + [vm((4,) + s, bf) for s in shapes]
         + [
             vm((16, 128, 768), bf),

time: 224 us -> 217 us (0.969)
  Pallas kernels: 221 us -> 215 us
    pallas_call x1, Pallas kernels: 132 us -> 121 us  [forward_call(): pl.pallas_call(forward_kernel, out_shape=outs, in_specs=[far, far, here,...]
    pallas_call x1, Pallas kernels: 86.2 us -> 90.9 us  [backward_call(): pl.pallas_call(backward_kernel, out_shape=outs, in_specs=[far] * 15, out_...]
where the time goes in v1:
time: 217 us
  Pallas kernels  215 us (99%)
    pallas_call x1, Pallas kernels, forward_call(): pl.pallas_call(forward_kernel, out_shape=outs, in_specs=[far, far, here,...  121 us
    pallas_call x1, Pallas kernels, backward_call(): pl.pallas_call(backward_kernel, out_shape=outs, in_specs=[far] * 15, out_...  90.9 us

profile of v1, /device:TPU:11, one launch (start us, length us, event | category | flops | bytes accessed | tf_op | source)
XLA Modules:
  0.0 217.2 jit_solution(6380356580956304270)
XLA Ops:
  0.6 1.3 stack.27.rows24
  2.0 121.3 %forward.1 = (f32[2,128,768]{2,1,0:T(8,128)}, f32[16,768]{1,0:T(8,128)}, bf16[2,128,768]{2,1,0:T(8,128)(2,1)}, bf16[8,128,192]{2,1,0:T(8,128)(2,1)}, bf16[2,2,96...) custom-call(bf16[2,128,768]{2,1,0:T(8,128)(2,1)} %tokens.1, ...), custom_call_target="tpu_custom_call" | custom-call | tf_op jit(solution)/shard_map/forward/pallas_call | solution.py:1208
  123.2 90.9 %backward.1 = (f32[2,128,768]{2,1,0:T(8,128)}, f32[24,768]{1,0:T(8,128)}, f32[24,3072]{1,0:T(8,128)}, f32[96,768]{1,0:T(8,128)}, f32[4,24,576]{2,1,0:T(8,128)}, /*index=5*/f32[8,128]{1,0:T(8,128)}) custom-call(bf16[8,128,192]{2,1,0:T(8,128)(2,1)} %get-tuple-element.51.dc_h, f32[2,128,768]{2,1,0:T(8,128)} %get-tuple-element.52.dr1, ...), custom_call_target="tpu_custom_call" | custom-call | tf_op jit(solution)/shard_map/backward/pallas_call | solution.py:1780
  214.1 2.9 %finish.1 = (bf16[2,128,768]{2,1,0:T(8,128)(2,1)}, f32[2,128,768]{2,1,0:T(8,128)}, f32[24,2304]{1,0:T(8,128)}, f32[24,768]{1,0:T(8,128)}, f32[24,3072]{1,0:T(8,1...) custom-call(bf16[2,128,768]{2,1,0:T(8,128)(2,1)} %get-tuple-element., ...), custom_call_target="tpu_custom_call" | custom-call | tf_op jit(solution)/shard_map/finish/pallas_call | solution.py:1811

commit v2 on v1

--- a/solution.py
+++ b/solution.py
@@ -1512,10 +1512,12 @@
             gvr[3 + z] = gv
 
     gv_stage(0)
+    stage2(0)
+    stage3(0)
     beside = {
-        0: ((stage2, 0), (stage3, 0)),
-        1: ((stage2, 1),),
-        2: ((stage2, 2), (stage3, 1)),
+        0: ((stage2, 1),),
+        1: ((stage2, 2), (stage3, 1)),
+        2: ((stage2, 3), (stage3, 2)),
     }
     for t in range(4):
         attend(t)
@@ -1530,8 +1532,7 @@
             [dks[hh, rows, :] for hh in range(3)] + [dvs[hh, rows, :] for hh in range(3)], axis=1
         ).astype(jnp.bfloat16)
     remote(kv_send, kv_recv, kv_ss, kv_rs, to_c).start()
-    stage2(3)
-    stage3(2)
+    stage3(3)
     wait_for(kv_recv, kv_rs)
 
     qsum = jnp.zeros((1, 192), jnp.float32)
@@ -1583,7 +1584,6 @@
                 base = (xs * 16 + hs * 4 + zz) * 24
                 gq[hs % 2, xs, zz // 2, 2 * (zz % 2) + hs // 2] = total[base : base + 24].astype(jnp.bfloat16)
     remote(gq.at[1 - c], gqc, gq_ss.at[0], gq_rs.at[0], to_c).start()
-    stage3(3)
     stage4(0)
 
     def add_qb(k):

time: 217 us -> 223 us (1.028)
  Pallas kernels: 215 us -> 220 us
    pallas_call x1, Pallas kernels: 90.9 us -> 96 us  [backward_call(): pl.pallas_call(backward_kernel, out_shape=outs, in_specs=[far] * 15, out_...]
where the time goes in v2:
time: 223 us; the launch traced here: 222 us
  Pallas kernels  220 us (99%)
    pallas_call x1, Pallas kernels, forward_call(): pl.pallas_call(forward_kernel, out_shape=outs, in_specs=[far, far, here,...  121 us
    pallas_call x1, Pallas kernels, backward_call(): pl.pallas_call(backward_kernel, out_shape=outs, in_specs=[far] * 15, out_...  96 us

profile of v2, /device:TPU:11, one launch (start us, length us, event | category | flops | bytes accessed | tf_op | source)
XLA Modules:
  0.0 222.4 jit_solution(10942363552269428687)
XLA Ops:
  0.6 1.3 stack.27.rows24
  2.0 121.3 %forward.1 = (f32[2,128,768]{2,1,0:T(8,128)}, f32[16,768]{1,0:T(8,128)}, bf16[2,128,768]{2,1,0:T(8,128)(2,1)}, bf16[8,128,192]{2,1,0:T(8,128)(2,1)}, bf16[2,2,96...) custom-call(bf16[2,128,768]{2,1,0:T(8,128)(2,1)} %tokens.1, ...), custom_call_target="tpu_custom_call" | custom-call | tf_op jit(solution)/shard_map/forward/pallas_call | solution.py:1208
  123.2 96.0 %backward.1 = (f32[2,128,768]{2,1,0:T(8,128)}, f32[24,768]{1,0:T(8,128)}, f32[24,3072]{1,0:T(8,128)}, f32[96,768]{1,0:T(8,128)}, f32[4,24,576]{2,1,0:T(8,128)}, /*index=5*/f32[8,128]{1,0:T(8,128)}) custom-call(bf16[8,128,192]{2,1,0:T(8,128)(2,1)} %get-tuple-element.51.dc_h, f32[2,128,768]{2,1,0:T(8,128)} %get-tuple-element.52.dr1, ...), custom_call_target="tpu_custom_call" | custom-call | tf_op jit(solution)/shard_map/backward/pallas_call | solution.py:1780
  219.3 2.9 %finish.1 = (bf16[2,128,768]{2,1,0:T(8,128)(2,1)}, f32[2,128,768]{2,1,0:T(8,128)}, f32[24,2304]{1,0:T(8,128)}, f32[24,768]{1,0:T(8,128)}, f32[24,3072]{1,0:T(8,1...) custom-call(bf16[2,128,768]{2,1,0:T(8,128)(2,1)} %get-tuple-element., ...), custom_call_target="tpu_custom_call" | custom-call | tf_op jit(solution)/shard_map/finish/pallas_call | solution.py:1811
